TPU v7x, 128 devices: a whole 4x4x4 slice. The times are simulated.
128 devices in a mesh: tp: 2 (over core), grp: 32 (over z, y, x_lo), rep: 2 (over x_hi).
Axes of the slice: x: 4 (x_hi: 2, x_lo: 2; x = x_hi * 2 + x_lo), y: 4, z: 4, core: 2. Of those that a mesh axis runs over, the one named last changes fastest.
Arguments:
- tokens: bfloat16 [8192, 4096], P(('rep', 'tp', 'grp')), parts along dimension 0, may hold values from -6 to 6
- qkv_weight: bfloat16 [4096, 5120], P(None, ('tp', 'grp')), may hold values from -0.09375 to 0.09375
- qkv_bias: bfloat16 [5120], replicated, may hold values from -3 to 3
- cache: bfloat16 [512, 1024, 1024], P(('rep', 'tp', 'grp')), parts along dimension 0, may hold values from -80 to 80
- lengths: int32 [512], P('rep'), parts along dimension 0, may hold values from 128 to 1024, as said below
- slot_stream: int32 [512], P('rep'), parts along dimension 0, may hold values from 0 to 255, each once
Outputs:
- attended: bfloat16 [8192, 4096], P(('rep', 'tp', 'grp')), parts along dimension 0
There are 2 independent parts, one for each index of `rep`. A program takes and returns all parts, laid end to end along the dimension named above; an argument that names none is the same for every part. Nothing has to cross between parts.
Inputs may be any that keep to these rules, and one draw needn't show every extreme that they name: `lengths`: cache length of each stream; some stream has exactly 1024 and some exactly 128. `slot_stream`: each stream appears in exactly one slot.
All inputs are finite; a program needn't handle non-finite values.
Results may differ from a plain program's by a relative error of at most 0.004.
The roundings to bfloat16 on the way count: a program that leaves them out, or rounds other values in their place, can miss the bound.
Values may be sent and summed in bfloat16 or wider, within the bound.
No kernel may reach another device: no remote copies, remote signals or barrier semaphores. Data moves between devices by JAX's collectives and lax.ppermute only.
A program may use at most 128 MiB of HBM per device.

v0:
```python
import jax
import jax.numpy as jnp
from jax import lax
from jax.sharding import PartitionSpec as P

HD = 128
HQ = 32
KVH = 4
STRETCH = 16
CAP = 1024
GROUP = 8
ROPE_THETA = 1000000.0


def rotate(vectors, positions):
    half_width = vectors.shape[-1] // 2
    frequency = ROPE_THETA ** (
        -(jnp.arange(half_width, dtype=jnp.float32) * 2.0) / vectors.shape[-1]
    )
    angles = positions.astype(jnp.float32)[:, None] * frequency[None, :]
    cosine = jnp.cos(angles)[:, None, :]
    sine_part = jnp.sin(angles)[:, None, :]
    front_half = vectors[..., :half_width]
    back_half = vectors[..., half_width:]
    return jnp.concatenate(
        [front_half * cosine - back_half * sine_part, back_half * cosine + front_half * sine_part],
        axis=-1,
    )


def attend(token_block, slot_cache, length):
    query_width = HQ * HD
    kv_width = KVH * HD
    positions = length + jnp.arange(STRETCH, dtype=jnp.int32)
    queries = rotate(
        token_block[:, :query_width].astype(jnp.float32).reshape(STRETCH, HQ, HD), positions
    ).astype(jnp.bfloat16)
    new_keys = rotate(
        token_block[:, query_width : query_width + kv_width]
        .astype(jnp.float32)
        .reshape(STRETCH, KVH, HD),
        positions,
    ).astype(jnp.bfloat16)
    new_values = token_block[:, query_width + kv_width :].reshape(STRETCH, KVH, HD)
    grouped = (
        queries.reshape(STRETCH, KVH, GROUP, HD)
        .transpose(1, 0, 2, 3)
        .reshape(KVH, STRETCH * GROUP, HD)
    )
    score_scale = HD ** (-0.5)
    query_token = jnp.arange(STRETCH * GROUP, dtype=jnp.int32) // GROUP
    scores = (
        jnp.einsum("krd,jkd->krj", grouped, new_keys, preferred_element_type=jnp.float32)
        * score_scale
    )
    causal = jnp.arange(STRETCH, dtype=jnp.int32)[None, :] <= query_token[:, None]
    scores = jnp.where(causal[None], scores, -jnp.inf)
    row_max = jnp.max(scores, axis=-1)
    exponent = jnp.exp(scores - row_max[..., None])
    row_total = jnp.sum(exponent, axis=-1)
    running = jnp.einsum(
        "krj,jkd->krd",
        exponent.astype(jnp.bfloat16),
        new_values,
        preferred_element_type=jnp.float32,
    )
    key_span = min(CAP, 256)
    key_part = slot_cache[:, :kv_width]
    value_part = slot_cache[:, kv_width:]

    def visit(block_index, running_state):
        old_max, old_total, old_sum = running_state
        offset = block_index * key_span
        key_block = lax.dynamic_slice_in_dim(key_part, offset, key_span, 0).reshape(
            key_span, KVH, HD
        )
        value_block = lax.dynamic_slice_in_dim(value_part, offset, key_span, 0).reshape(
            key_span, KVH, HD
        )
        block_scores = (
            jnp.einsum("krd,jkd->krj", grouped, key_block, preferred_element_type=jnp.float32)
            * score_scale
        )
        in_cache = offset + jnp.arange(key_span, dtype=jnp.int32) < length
        block_scores = jnp.where(in_cache[None, None, :], block_scores, -jnp.inf)
        new_max = jnp.maximum(old_max, jnp.max(block_scores, axis=-1))
        rescale = jnp.exp(old_max - new_max)
        block_exp = jnp.exp(block_scores - new_max[..., None])
        new_total = old_total * rescale + jnp.sum(block_exp, axis=-1)
        new_sum = old_sum * rescale[..., None] + jnp.einsum(
            "krj,jkd->krd",
            block_exp.astype(jnp.bfloat16),
            value_block,
            preferred_element_type=jnp.float32,
        )
        return (new_max, new_total, new_sum)

    block_count = CAP // key_span
    row_max, row_total, running = lax.fori_loop(
        0, block_count, visit, (row_max, row_total, running)
    )
    result = running / row_total[..., None]
    return (
        result.reshape(KVH, STRETCH, GROUP, HD)
        .transpose(1, 0, 2, 3)
        .reshape(STRETCH, HQ * HD)
        .astype(jnp.bfloat16)
    )


def on_device(tokens, qkv_weight, qkv_bias, cache, lengths, slot_stream):
    my_index = lax.axis_index(("tp", "grp"))
    grp_index = lax.axis_index("grp")
    tp_count = lax.axis_size("tp")
    grp_count = lax.axis_size("grp")
    per_device = cache.shape[0]
    local_rows = per_device * STRETCH
    shard_cols = qkv_weight.shape[1]
    weight_cols = lax.all_gather(qkv_weight, "tp", axis=1, tiled=True)
    bias_table = qkv_bias.reshape(tp_count, grp_count, shard_cols)
    bias_cols = (
        lax.dynamic_index_in_dim(bias_table, grp_index, 1, keepdims=False)
        .reshape(-1)
        .astype(jnp.float32)
    )
    partial_cols = jnp.dot(
        lax.all_gather(tokens, "grp", axis=0, tiled=True),
        weight_cols,
        preferred_element_type=jnp.float32,
    )
    rounded_cols = (partial_cols + bias_cols[None, :]).astype(jnp.bfloat16)
    received = lax.all_to_all(rounded_cols, "grp", split_axis=0, concat_axis=1, tiled=True)
    projected_qkv = (
        received.reshape(local_rows, grp_count, tp_count, shard_cols)
        .transpose(0, 2, 1, 3)
        .reshape(local_rows, -1)
    )
    my_slots = my_index * per_device + jnp.arange(per_device, dtype=jnp.int32)
    my_lengths = jnp.take(lengths, jnp.take(slot_stream, my_slots))
    attended = jnp.concatenate(
        [
            attend(
                projected_qkv[slot_index * STRETCH : (slot_index + 1) * STRETCH],
                cache[slot_index],
                my_lengths[slot_index],
            )
            for slot_index in range(per_device)
        ],
        axis=0,
    )
    return attended


def solution(mesh):
    in_specs = (
        P(("rep", "tp", "grp"), None),
        P(None, ("tp", "grp")),
        P(),
        P(("rep", "tp", "grp"), None, None),
        P("rep"),
        P("rep"),
    )
    out_specs = P(("rep", "tp", "grp"), None)
    return jax.shard_map(
        on_device, mesh=mesh, in_specs=in_specs, out_specs=out_specs, check_vma=False
    )
```

profile of v0, /device:TPU:0, one launch (start us, length us, event | category | flops | bytes accessed | tf_op | source)
XLA Modules:
  0.0 482.9 jit_solution(10885012108823817912)
XLA Ops:
  8.9 5.6 %fusion.89 = (bf16[1,1024,1024]{2,1,0:T(8,128)(2,1)}, bf16[1,1024,1024]{2,1,0:T(8,128)(2,1)}, bf16[1,1024,1024]{2,1,0:T(8,128)(2,1)}, bf16[1,1024,1024]{2,1,0:T(8,128)(2,1)S(1)}) fusion(bf16[4,1024,1024]{2,1,0:T(8,128)(2,1)} %param.19), kind=kLoop, calls=%fused_computation.195 | loop fusion | bytes 16777216 | tf_op jit(solution)/shard_map/slice | solution.py:144
  14.6 2.6 copy.114
  17.1 2.9 copy.111
  24.7 3.0 fusion.93
  27.8 1.5 fusion.92
  29.3 361.1 %all-gather.3.cloned.1.call-done = bf16[2048,4096]{1,0:T(8,128)(2,1)} async-done(((bf16[64,4096]{1,0:T(8,128)(2,1)}), bf16[2048,4096]{1,0:T(8,128)(2,1)}) %all-gather.3.cloned.1.call-update) | async-done | bytes 16777232 | tf_op jit(solution)/shard_map/all_gather | solution.py:127
  390.4 11.8 %fusion.24 = bf16[2048,160]{0,1:T(8,128)(2,1)S(1)} fusion(bf16[2048,4096]{1,0:T(8,128)(2,1)} %all-gather.3.cloned.1.call-done, bf16[4096,160]{0,1:T(8,128)(2,1)} %all-gather.5.cloned.1.call-done, f32[160]{0:T(256)S(1)} %reshape.502), kind=kOutput, calls=%fused_computation.55 | convolution fusion | flops 2685009920 | bytes 18743936 | tf_op jit(solution)/shard_map/dot_general | solution.py:126
  402.2 1.3 copy.102
  403.5 4.9 %all-to-all-start = ((bf16[32,64,160]{2,1,0:T(8,128)(2,1)}), bf16[32,64,160]{2,1,0:T(8,128)(2,1)}, u32[]{:S(2)}, u32[]{:S(2)}) async-start(bf16[32,64,160]{2,1,0:T(8,128)(2,1)} %bitcast.12), calls=%async_computation | async-start | bytes 2097152 | tf_op jit(solution)/shard_map/all_to_all | solution.py:132
  408.4 2.6 copy.108
  410.9 2.9 copy.105
  413.8 3.0 fusion.91
  416.8 1.1 fusion.90
  418.0 8.1 %all-to-all-done = bf16[32,64,160]{2,1,0:T(8,128)(2,1)} async-done(((bf16[32,64,160]{2,1,0:T(8,128)(2,1)}), bf16[32,64,160]{2,1,0:T(8,128)(2,1)}, u32[]{:S(2)}, u32[]{:S(2)}) %all-to-all-start) | async-done | bytes 655392 | tf_op jit(solution)/shard_map/all_to_all | solution.py:132
  426.1 1.6 reshape.477
  427.7 1.2 copy.180
  431.9 10.3 %while.71 = (s32[]{:T(128)}, f32[4,128]{1,0:T(4,128)S(1)}, f32[4,128]{1,0:T(4,128)S(1)}, f32[4,128,128]{2,1,0:T(8,128)S(1)}, s32[]{:T(128)}, /*index=5*/bf16[102...) while((s32[]{:T(128)}, f32[4,128]{1,0:T(4,128)S(1)}, ...), condition=%wide.region_23.25_spmd, body=%wide.region_20.24_spmd.sunk | while | flops 68158976 | bytes 3834551 | solution.py:99
  431.9 1.1 constant_dynamic-slice_fusion.15
  434.4 1.1 constant_dynamic-slice_fusion.15
  437.0 1.1 constant_dynamic-slice_fusion.15
  439.6 1.1 constant_dynamic-slice_fusion.15
  443.1 9.8 %while.70 = (s32[]{:T(128)}, f32[4,128]{1,0:T(4,128)S(1)}, f32[4,128]{1,0:T(4,128)S(1)}, f32[4,128,128]{2,1,0:T(8,128)S(1)}, s32[]{:T(128)}, /*index=5*/bf16[102...) while((s32[]{:T(128)}, f32[4,128]{1,0:T(4,128)S(1)}, ...), condition=%wide.region_17.19_spmd, body=%wide.region_14.18_spmd.sunk | while | flops 68158976 | bytes 3834551 | solution.py:99
  443.1 1.1 constant_dynamic-slice_fusion.14
  445.5 1.1 constant_dynamic-slice_fusion.14
  448.0 1.1 constant_dynamic-slice_fusion.14
  450.5 1.1 constant_dynamic-slice_fusion.14
  454.4 9.7 %while.69 = (s32[]{:T(128)}, f32[4,128]{1,0:T(4,128)S(1)}, f32[4,128]{1,0:T(4,128)S(1)}, f32[4,128,128]{2,1,0:T(8,128)S(1)}, s32[]{:T(128)}, /*index=5*/bf16[102...) while((s32[]{:T(128)}, f32[4,128]{1,0:T(4,128)S(1)}, ...), condition=%wide.region_11.13_spmd, body=%wide.region_8.12_spmd.sunk | while | flops 68158976 | bytes 3834551 | solution.py:99
  454.5 1.1 constant_dynamic-slice_fusion.13
  456.9 1.1 constant_dynamic-slice_fusion.13
  459.3 1.1 constant_dynamic-slice_fusion.13
  461.8 1.1 constant_dynamic-slice_fusion.13
  465.1 9.8 %while.68 = (s32[]{:T(128)}, f32[4,128]{1,0:T(4,128)S(1)}, f32[4,128]{1,0:T(4,128)S(1)}, f32[4,128,128]{2,1,0:T(8,128)S(1)}, s32[]{:T(128)}, /*index=5*/bf16[102...) while((s32[]{:T(128)}, f32[4,128]{1,0:T(4,128)S(1)}, ...), condition=%wide.region_5.7_spmd, body=%wide.region_2.6_spmd.sunk | while | flops 68158976 | bytes 3834551 | solution.py:99
  (206 shorter events, 39.9 us)
Async XLA Ops:
  6.5 13.5 %copy-start = (s32[256]{0:T(256)S(1)}, s32[256]{0:T(256)}, u32[]{:S(2)}) copy-start(s32[256]{0:T(256)} %param.21) | copy-start | bytes 3076
  6.5 22.7 %all-gather.5.cloned.1.call-start = ((), (), s32[]{:S(2)}) async-start(), calls=%async_computation.2 | async-start | bytes 1966080 | tf_op jit(solution)/shard_map/all_gather | solution.py:119
  7.3 383.1 %all-gather.3.cloned.1.call-start = ((), (), s32[]{:S(2)}) async-start(), calls=%async_computation.1 | async-start | bytes 17301504 | tf_op jit(solution)/shard_map/all_gather | solution.py:127
  17.1 3.6 copy-start.2
  402.2 6.2 %copy-start.3 = (bf16[1,1024,1024]{2,1,0:T(8,128)(2,1)S(1)}, bf16[1,1024,1024]{2,1,0:T(8,128)(2,1)}, u32[]{:S(2)}) copy-start(bf16[1,1024,1024]{2,1,0:T(8,128)(2,1)} %get-tuple-element.664) | copy-start | bytes 6291460
  403.5 22.6 %all-to-all-start = ((bf16[32,64,160]{2,1,0:T(8,128)(2,1)}), bf16[32,64,160]{2,1,0:T(8,128)(2,1)}, u32[]{:S(2)}, u32[]{:S(2)}) async-start(bf16[32,64,160]{2,1,0:T(8,128)(2,1)} %bitcast.12), calls=%async_computation | async-start | bytes 2097152 | tf_op jit(solution)/shard_map/all_to_all | solution.py:132
  474.9 1.1 copy-start.1
Sparse Core Ops, SparseCore 0:
  9.0 14.5 all-gather.4
  25.2 365.1 all-gather.2
where the time goes:
time: 484 us; the launch traced here: 483 us
  waiting for transfers between devices  371 us (77%)
  local copies, waits for them, and re-layouts  51.5 us (11%)
  matrix products  23.9 us (5%)
  other arithmetic  17 us (4%)
  between operations  13.9 us (3%)
  starting transfers between devices  4.9 us (1%)
    all_gather x1, waiting for transfers between devices, on_device(): lax.all_gather(tokens, 'grp', axis=0, tiled=True)  361 us
    dynamic_slice x16, local copies, waits for them, and re-layouts, visit(): lax.dynamic_slice_in_dim(value_part, offset, key_span, 0)  16.9 us
    dot_general x1, matrix products, on_device(): jnp.dot(lax.all_gather(tokens, 'grp', axis=0, tiled=True), weight_cols, p...  11.8 us
    unnamed x20, local copies, waits for them, and re-layouts  11.3 us
    lt x16, other arithmetic, visit(): in_cache = offset + jnp.arange(key_span, dtype=jnp.int32) < length  9.86 us
  transfers between devices with their start and end apart: 3, of which 2 were waited for; matrix products, arithmetic and copies ran while one was open for 6% of the time, Pallas kernels for 0%

commit v1 on v0

--- a/solution.py
+++ b/solution.py
@@ -124,7 +124,9 @@
         .astype(jnp.float32)
     )
     partial_cols = jnp.dot(
-        lax.all_gather(tokens, "grp", axis=0, tiled=True),
+        jnp.concatenate(
+            lax.all_to_all(jnp.stack([tokens] * lax.axis_size("grp")), "grp", 0, 0), axis=0
+        ),
         weight_cols,
         preferred_element_type=jnp.float32,
     )

time: 484 us -> 406 us (0.84)
  waiting for transfers between devices: 371 us -> 236 us
  starting transfers between devices: 4.9 us -> 55.5 us
  local copies, waits for them, and re-layouts: 51.5 us -> 57.7 us
    all_gather x1 -> x0, waiting for transfers between devices: 361 us -> none  [on_device(): lax.all_gather(tokens, 'grp', axis=0, tiled=True)]
    all_to_all x0 -> x1, waiting for transfers between devices: none -> 229 us  [on_device(): lax.all_to_all(jnp.stack([tokens] * lax.axis_size('grp')), 'grp', 0, 0)]
    all_to_all x1, starting transfers between devices: 4.86 us -> 45.8 us  [on_device(): lax.all_to_all(rounded_cols, 'grp', split_axis=0, concat_axis=1, tiled=True)]
    all_to_all x0 -> x1, starting transfers between devices: none -> 9.61 us  [on_device(): lax.all_to_all(jnp.stack([tokens] * lax.axis_size('grp')), 'grp', 0, 0)]
    another operation x0 -> x1, local copies, waits for them, and re-layouts: none -> 6.74 us  [on_device(): jnp.stack([tokens] * lax.axis_size('grp'))]
    unnamed x20 -> x22, local copies, waits for them, and re-layouts: 11.3 us -> 11.4 us
  transfers between devices with their start and end apart: 3 -> 3, of which waited for: 2 -> 2; matrix products, arithmetic and copies ran while one was open for 6% -> 7% of each run, Pallas kernels for 0% -> 0%
where the time goes in v1:
time: 406 us; the launch traced here: 405 us
  waiting for transfers between devices  236 us (58%)
  local copies, waits for them, and re-layouts  57.7 us (14%)
  starting transfers between devices  55.5 us (14%)
  matrix products  23.9 us (6%)
  other arithmetic  16.9 us (4%)
  between operations  13.9 us (3%)
    all_to_all x1, waiting for transfers between devices, on_device(): lax.all_to_all(jnp.stack([tokens] * lax.axis_size('grp')), 'grp', 0, 0)  229 us
    all_to_all x1, starting transfers between devices, on_device(): lax.all_to_all(rounded_cols, 'grp', split_axis=0, concat_axis=1, tiled=True)  45.8 us
    dynamic_slice x16, local copies, waits for them, and re-layouts, visit(): lax.dynamic_slice_in_dim(value_part, offset, key_span, 0)  16.9 us
    dot_general x1, matrix products, on_device(): jnp.dot(jnp.concatenate(lax.all_to_all(jnp.stack([tokens] * lax.axis_size...  11.8 us
    unnamed x22, local copies, waits for them, and re-layouts  11.4 us
    lt x16, other arithmetic, visit(): in_cache = offset + jnp.arange(key_span, dtype=jnp.int32) < length  9.74 us
    all_to_all x1, starting transfers between devices, on_device(): lax.all_to_all(jnp.stack([tokens] * lax.axis_size('grp')), 'grp', 0, 0)  9.61 us
    slice x4, local copies, waits for them, and re-layouts, attend(): value_part = slot_cache[:, kv_width:]  8.68 us
  transfers between devices with their start and end apart: 3, of which 2 were waited for; matrix products, arithmetic and copies ran while one was open for 7% of the time, Pallas kernels for 0%

profile of v1, /device:TPU:0, one launch (start us, length us, event | category | flops | bytes accessed | tf_op | source)
XLA Modules:
  0.0 405.1 jit_solution(2733757657523378965)
XLA Ops:
  6.5 6.7 %stack.2 = bf16[32,64,4096]{2,1,0:T(8,128)(2,1)} broadcast(bf16[64,4096]{1,0:T(8,128)(2,1)} %param.16), dimensions={1,2} | broadcast | bytes 17301504 | tf_op jit(solution)/shard_map/stack | solution.py:128
  13.3 9.6 %all-to-all-start = ((bf16[32,64,4096]{2,1,0:T(8,128)(2,1)}), bf16[32,64,4096]{2,1,0:T(8,128)(2,1)}, u32[]{:S(2)}, u32[]{:S(2)}) async-start(bf16[32,64,4096]{2,1,0:T(8,128)(2,1)} %stack.2), calls=%async_computation | async-start | bytes 33554432 | tf_op jit(solution)/shard_map/all_to_all | solution.py:128
  25.7 5.8 %fusion.89 = (bf16[1,1024,1024]{2,1,0:T(8,128)(2,1)}, bf16[1,1024,1024]{2,1,0:T(8,128)(2,1)}, bf16[1,1024,1024]{2,1,0:T(8,128)(2,1)}, bf16[1,1024,1024]{2,1,0:T(8,128)(2,1)S(1)}) fusion(bf16[4,1024,1024]{2,1,0:T(8,128)(2,1)} %param.19), kind=kLoop, calls=%fused_computation.195 | loop fusion | bytes 16777216 | tf_op jit(solution)/shard_map/slice | solution.py:146
  31.7 2.6 copy.114
  34.2 3.0 copy.111
  39.9 3.0 fusion.93
  42.9 1.5 fusion.92
  44.4 228.7 %all-to-all-done = bf16[32,64,4096]{2,1,0:T(8,128)(2,1)} async-done(((bf16[32,64,4096]{2,1,0:T(8,128)(2,1)}), bf16[32,64,4096]{2,1,0:T(8,128)(2,1)}, u32[]{:S(2)}, u32[]{:S(2)}) %all-to-all-start) | async-done | bytes 16777248 | tf_op jit(solution)/shard_map/all_to_all | solution.py:128
  273.1 11.8 %fusion.24 = bf16[2048,160]{0,1:T(8,128)(2,1)S(1)} fusion(bf16[2048,4096]{1,0:T(8,128)(2,1)} %bitcast.12, bf16[4096,160]{0,1:T(8,128)(2,1)} %all-gather.2.cloned.1.call-done, f32[160]{0:T(256)S(1)} %reshape.508), kind=kOutput, calls=%fused_computation.55 | convolution fusion | flops 2685009920 | bytes 18743936 | tf_op jit(solution)/shard_map/dot_general | solution.py:126
  284.9 1.3 copy.102
  286.2 45.8 %all-to-all-start.1 = ((bf16[32,64,160]{2,1,0:T(8,128)(2,1)}), bf16[32,64,160]{2,1,0:T(8,128)(2,1)}, u32[]{:S(2)}, u32[]{:S(2)}) async-start(bf16[32,64,160]{2,1,0:T(8,128)(2,1)} %bitcast.13), calls=%async_computation.1 | async-start | bytes 2097152 | tf_op jit(solution)/shard_map/all_to_all | solution.py:134
  332.0 2.6 copy.108
  334.6 2.9 copy.105
  337.5 3.0 fusion.91
  340.5 1.1 fusion.90
  341.6 6.8 %all-to-all-done.1 = bf16[32,64,160]{2,1,0:T(8,128)(2,1)} async-done(((bf16[32,64,160]{2,1,0:T(8,128)(2,1)}), bf16[32,64,160]{2,1,0:T(8,128)(2,1)}, u32[]{:S(2)}, u32[]{:S(2)}) %all-to-all-start.1) | async-done | bytes 655392 | tf_op jit(solution)/shard_map/all_to_all | solution.py:134
  348.5 1.6 reshape.483
  350.1 1.2 copy.180
  354.2 9.8 %while.71 = (s32[]{:T(128)}, f32[4,128]{1,0:T(4,128)S(1)}, f32[4,128]{1,0:T(4,128)S(1)}, f32[4,128,128]{2,1,0:T(8,128)S(1)}, s32[]{:T(128)}, /*index=5*/bf16[102...) while((s32[]{:T(128)}, f32[4,128]{1,0:T(4,128)S(1)}, ...), condition=%wide.region_23.25_spmd, body=%wide.region_20.24_spmd.sunk | while | flops 68158976 | bytes 3834551 | solution.py:99
  354.2 1.1 constant_dynamic-slice_fusion.15
  356.7 1.1 constant_dynamic-slice_fusion.15
  359.1 1.1 constant_dynamic-slice_fusion.15
  361.6 1.1 constant_dynamic-slice_fusion.15
  364.9 10.3 %while.70 = (s32[]{:T(128)}, f32[4,128]{1,0:T(4,128)S(1)}, f32[4,128]{1,0:T(4,128)S(1)}, f32[4,128,128]{2,1,0:T(8,128)S(1)}, s32[]{:T(128)}, /*index=5*/bf16[102...) while((s32[]{:T(128)}, f32[4,128]{1,0:T(4,128)S(1)}, ...), condition=%wide.region_17.19_spmd, body=%wide.region_14.18_spmd.sunk | while | flops 68158976 | bytes 3834551 | solution.py:99
  364.9 1.1 constant_dynamic-slice_fusion.14
  367.5 1.1 constant_dynamic-slice_fusion.14
  370.1 1.1 constant_dynamic-slice_fusion.14
  372.7 1.1 constant_dynamic-slice_fusion.14
  376.8 10.0 %while.69 = (s32[]{:T(128)}, f32[4,128]{1,0:T(4,128)S(1)}, f32[4,128]{1,0:T(4,128)S(1)}, f32[4,128,128]{2,1,0:T(8,128)S(1)}, s32[]{:T(128)}, /*index=5*/bf16[102...) while((s32[]{:T(128)}, f32[4,128]{1,0:T(4,128)S(1)}, ...), condition=%wide.region_11.13_spmd, body=%wide.region_8.12_spmd.sunk | while | flops 68158976 | bytes 3834551 | solution.py:99
  376.8 1.1 constant_dynamic-slice_fusion.13
  384.3 1.1 constant_dynamic-slice_fusion.13
  387.7 9.5 %while.68 = (s32[]{:T(128)}, f32[4,128]{1,0:T(4,128)S(1)}, f32[4,128]{1,0:T(4,128)S(1)}, f32[4,128,128]{2,1,0:T(8,128)S(1)}, s32[]{:T(128)}, /*index=5*/bf16[102...) while((s32[]{:T(128)}, f32[4,128]{1,0:T(4,128)S(1)}, ...), condition=%wide.region_5.7_spmd, body=%wide.region_2.6_spmd.sunk | while | flops 68158976 | bytes 3834551 | solution.py:99
  (208 shorter events, 40.5 us)
Async XLA Ops:
  6.5 17.1 %copy-start = (s32[256]{0:T(256)S(1)}, s32[256]{0:T(256)}, u32[]{:S(2)}) copy-start(s32[256]{0:T(256)} %param.21) | copy-start | bytes 3076
  13.3 11.1 %copy-start.2 = (s32[256]{0:T(256)S(1)}, s32[256]{0:T(256)}, u32[]{:S(2)}) copy-start(s32[256]{0:T(256)} %param.20) | copy-start | bytes 3076
  13.3 259.8 %all-to-all-start = ((bf16[32,64,4096]{2,1,0:T(8,128)(2,1)}), bf16[32,64,4096]{2,1,0:T(8,128)(2,1)}, u32[]{:S(2)}, u32[]{:S(2)}) async-start(bf16[32,64,4096]{2,1,0:T(8,128)(2,1)} %stack.2), calls=%async_computation | async-start | bytes 33554432 | tf_op jit(solution)/shard_map/all_to_all | solution.py:128
  22.9 21.5 %all-gather.2.cloned.1.call-start = ((), (), s32[]{:S(2)}) async-start(), calls=%async_computation.2 | async-start | bytes 1966080 | tf_op jit(solution)/shard_map/all_gather | solution.py:119
  25.7 5.8 %copy-start.4 = (bf16[5120]{0:T(1024)(128)(2,1)S(1)}, bf16[5120]{0:T(1024)(128)(2,1)}, u32[]{:S(2)}) copy-start(bf16[5120]{0:T(1024)(128)(2,1)} %param.18) | copy-start | bytes 30724
  284.9 47.2 %copy-start.3 = (bf16[1,1024,1024]{2,1,0:T(8,128)(2,1)S(1)}, bf16[1,1024,1024]{2,1,0:T(8,128)(2,1)}, u32[]{:S(2)}) copy-start(bf16[1,1024,1024]{2,1,0:T(8,128)(2,1)} %get-tuple-element.664) | copy-start | bytes 6291460
  286.2 62.3 %all-to-all-start.1 = ((bf16[32,64,160]{2,1,0:T(8,128)(2,1)}), bf16[32,64,160]{2,1,0:T(8,128)(2,1)}, u32[]{:S(2)}, u32[]{:S(2)}) async-start(bf16[32,64,160]{2,1,0:T(8,128)(2,1)} %bitcast.13), calls=%async_computation.1 | async-start | bytes 2097152 | tf_op jit(solution)/shard_map/all_to_all | solution.py:134
  397.2 1.1 copy-start.1
Sparse Core Ops, SparseCore 0:
  25.4 13.1 all-gather.1
